TPU v7x, 32 devices: a whole 2x2x4 slice. The times are simulated.
32 devices in a mesh: dp: 4 (over x, core), ctx: 8 (over z, y).
Axes of the slice: x: 2, y: 2, z: 4, core: 2. Of those that a mesh axis runs over, the one named last changes fastest.
Arguments:
- tokens: bfloat16 [4, 2048, 1024], P('dp', 'ctx'), may hold values from -6 to 6
- log_decay: float32 [4, 8, 2048], P('dp', None, 'ctx'), may hold values from -2.2 to 0
- lengths: int32 [4, 2], P('dp'), may hold values from 1 to 1280, 2048 in all within a row
- label_ids: int32 [4, 2048], P('dp', 'ctx'), may hold values from 0 to 511
- w_query: bfloat16 [1024, 1024], replicated, may hold values from -0.1875 to 0.1875
- w_key: bfloat16 [1024, 1024], replicated, may hold values from -0.1875 to 0.1875
- w_value: bfloat16 [1024, 1024], replicated, may hold values from -0.1875 to 0.1875
- norm_gain: float32 [1024], replicated, may hold values from 0.1 to 1.9
- label_query: bfloat16 [512, 1024], replicated, may hold values from -24 to 24
- label_weight: bfloat16 [512, 1024], replicated, may hold values from -0.75 to 0.75
Outputs:
- retention_out: bfloat16 [4, 2048, 1024], P('dp', 'ctx')
- logits: float32 [4, 2, 512], P('dp')
- recording_loss: float32 [4, 2], P('dp')
- mean_loss: float32 [], replicated
Inputs may be any that keep to these rules, and one draw needn't show every extreme that they name: Row g lists the lengths of the 2 recordings packed in order into the 2048 tokens of group g; they sum to 2048.
All inputs are finite; a program needn't handle non-finite values.
Results may differ from a plain program's by a relative error of at most 0.0058.
The roundings to bfloat16 on the way count: a program that leaves them out, or rounds other values in their place, can miss the bound.
Values sent between devices are 32-bit elements; how exact they have to be, the bound alone decides.
A program may use at most 128 MiB of HBM per device.

v0:
```python
import jax
import jax.numpy as jnp
from jax import lax
from jax.sharding import PartitionSpec as P

NEG_FILL = -1e30


def passed_along(x, axis, by):
    count = lax.axis_size(axis)
    pairs = [(i, i + by) for i in range(count) if 0 <= i + by < count]
    return lax.ppermute(x, axis, pairs)


def record_ids(length_row, positions):
    starts = jnp.cumsum(length_row) - length_row
    return jnp.sum((starts[:, None] <= positions[None, :]).astype(jnp.int32), axis=0) - 1


def local(
    tokens,
    log_decay,
    lengths,
    label_ids,
    w_query,
    w_key,
    w_value,
    norm_gain,
    label_query,
    label_weight,
):
    tok_rows = tokens.shape[1]
    model_width = tokens.shape[2]
    head_count = log_decay.shape[1]
    head_dim = model_width // head_count
    qk_scale = head_dim ** (-0.5)
    record_count = lengths.shape[1]
    label_count = label_query.shape[0]
    shard_start = lax.axis_index("ctx") * tok_rows
    local_pos = jnp.arange(tok_rows, dtype=jnp.int32)
    record = record_ids(lengths[0], shard_start + local_pos)
    before_rec = record_ids(lengths[0], jnp.reshape(shard_start - 1, (1,)))[0]
    features = tokens[0]
    queries = jnp.dot(features, w_query, preferred_element_type=jnp.float32).astype(jnp.bfloat16)
    key_rows = jnp.dot(features, w_key, preferred_element_type=jnp.float32).astype(jnp.bfloat16)
    value_rows = jnp.dot(features, w_value, preferred_element_type=jnp.float32).astype(jnp.bfloat16)
    decay_cum = jnp.cumsum(log_decay[0], axis=1)
    pair_mask = (local_pos[:, None] >= local_pos[None, :]) & (record[:, None] == record[None, :])
    linked = record == before_rec
    tail_rec = record == record[tok_rows - 1]

    def local_head(head_idx):
        q_head = lax.dynamic_slice_in_dim(queries, head_idx * head_dim, head_dim, 1)
        k_head = lax.dynamic_slice_in_dim(key_rows, head_idx * head_dim, head_dim, 1)
        v_head = lax.dynamic_slice_in_dim(value_rows, head_idx * head_dim, head_dim, 1)
        cum_head = lax.dynamic_index_in_dim(decay_cum, head_idx, 0, keepdims=False)
        scores = (
            jnp.einsum("td,sd->ts", q_head, k_head, preferred_element_type=jnp.float32) * qk_scale
        )
        decay_pair = jnp.exp(jnp.minimum(cum_head[:, None] - cum_head[None, :], 0.0))
        weights = jnp.where(pair_mask, scores * decay_pair, 0.0).astype(jnp.bfloat16)
        intra_sum = jnp.dot(weights, v_head, preferred_element_type=jnp.float32)
        k_decayed = (
            k_head.astype(jnp.float32)
            * jnp.where(tail_rec, jnp.exp(cum_head[tok_rows - 1] - cum_head), 0.0)[:, None]
        ).astype(jnp.bfloat16)
        local_state = jnp.dot(k_decayed.T, v_head, preferred_element_type=jnp.float32)
        carry_factor = jnp.where(linked[tok_rows - 1], jnp.exp(cum_head[tok_rows - 1]), 0.0)
        return (intra_sum, local_state, carry_factor)

    intra_all, local_state, carry_factor = lax.map(
        local_head, jnp.arange(head_count, dtype=jnp.int32)
    )

    def relay(turn_index, pair_state):
        outgoing, incoming = pair_state
        received = passed_along(outgoing, "ctx", 1)
        return (carry_factor[:, None, None] * received + local_state, received)

    outgoing, incoming = lax.fori_loop(
        0, lax.axis_size("ctx") - 1, relay, (local_state, jnp.zeros_like(local_state))
    )

    def finish_head(inputs):
        head_idx, intra_head, state_head = inputs
        q_head = lax.dynamic_slice_in_dim(queries, head_idx * head_dim, head_dim, 1)
        cum_head = lax.dynamic_index_in_dim(decay_cum, head_idx, 0, keepdims=False)
        q_decayed = q_head.astype(jnp.float32) * jnp.where(linked, jnp.exp(cum_head), 0.0)[:, None]
        total_out = (
            intra_head + jnp.dot(q_decayed, state_head, precision=lax.Precision.HIGH) * qk_scale
        )
        centred = total_out - jnp.mean(total_out, axis=1, keepdims=True)
        variance = jnp.mean(centred * centred, axis=1, keepdims=True)
        gain_head = lax.dynamic_slice_in_dim(norm_gain, head_idx * head_dim, head_dim, 0)
        return centred * lax.rsqrt(variance + 1e-05) * gain_head[None, :]

    normed = lax.map(finish_head, (jnp.arange(head_count, dtype=jnp.int32), intra_all, incoming))
    out_rows = jnp.transpose(normed, (1, 0, 2)).reshape(tok_rows, model_width).astype(jnp.bfloat16)
    member = record[None, :] == jnp.arange(record_count, dtype=jnp.int32)[:, None]
    member_float = member.astype(jnp.float32)

    def pool_head(head_idx):
        k_head = lax.dynamic_slice_in_dim(features, head_idx * head_dim, head_dim, 1)
        q_label = lax.dynamic_slice_in_dim(label_query, head_idx * head_dim, head_dim, 1)
        y_head = lax.dynamic_slice_in_dim(out_rows, head_idx * head_dim, head_dim, 1)
        w_head = lax.dynamic_slice_in_dim(label_weight, head_idx * head_dim, head_dim, 1)
        scores = (
            jnp.einsum("ld,td->lt", q_label, k_head, preferred_element_type=jnp.float32) * qk_scale
        )
        maxima = jnp.max(jnp.where(member[:, None, :], scores[None, :, :], NEG_FILL), axis=2)
        maxima_tok = jnp.sum(jnp.where(member[:, None, :], maxima[:, :, None], 0.0), axis=0)
        pool_weight = jnp.exp(scores - maxima_tok)
        label_value = jnp.einsum("ld,td->lt", w_head, y_head, preferred_element_type=jnp.float32)
        mass_part = jnp.einsum(
            "lt,rt->rl", pool_weight, member_float, precision=lax.Precision.HIGHEST
        )
        weighted = jnp.einsum(
            "lt,rt->rl", pool_weight * label_value, member_float, precision=lax.Precision.HIGHEST
        )
        return (maxima, mass_part, weighted)

    maxima, mass_part, weighted = lax.map(pool_head, jnp.arange(head_count, dtype=jnp.int32))
    label_hot = (label_ids[0][:, None] == jnp.arange(label_count, dtype=jnp.int32)[None, :]).astype(
        jnp.bfloat16
    )
    counts = jnp.dot(member.astype(jnp.bfloat16), label_hot, preferred_element_type=jnp.float32)
    top_score = lax.pmax(maxima, "ctx")
    rescale = jnp.exp(maxima - top_score)
    mass_all, weighted_all, counts_all = lax.psum(
        (mass_part * rescale, weighted * rescale, counts), "ctx"
    )
    logits = jnp.sum(weighted_all / mass_all, axis=0)
    target = (counts_all + 0.5) / (lengths[0].astype(jnp.float32)[:, None] + 1.0)
    rec_loss = jnp.mean(jax.nn.softplus(logits) - target * logits, axis=1)
    mean_loss = lax.psum(jnp.sum(rec_loss), "dp") / (lax.axis_size("dp") * record_count)
    return (out_rows[None], logits[None], rec_loss[None], mean_loss)


def solution(mesh):
    return jax.shard_map(
        local,
        mesh=mesh,
        in_specs=(
            P("dp", "ctx", None),
            P("dp", None, "ctx"),
            P("dp", None),
            P("dp", "ctx"),
            P(),
            P(),
            P(),
            P(),
            P(),
            P(),
        ),
        out_specs=(P("dp", "ctx", None), P("dp", None, None), P("dp", None), P()),
        check_vma=False,
    )
```

profile of v0, /device:TPU:0, one launch (start us, length us, event | category | flops | bytes accessed | tf_op | source)
XLA Modules:
  0.0 420.6 jit_solution(18007443025613736233)
XLA Ops:
  13.1 2.7 convolution_convert_fusion.2
  19.6 74.5 %while.55 = (s32[]{:T(128)}, f32[8,256,128]{2,1,0:T(8,128)}, f32[8,128,128]{2,1,0:T(8,128)S(1)}, f32[8]{0:T(128)S(1)}, s32[8]{0:T(128)S(1)}, /*index=5*/bf16[256...) while((s32[]{:T(128)}, f32[8,256,128]{2,1,0:T(8,128)}, ...), condition=%wide.region_6.7_spmd.clone, body=%wide.region_5.6_spmd.clone.sunk | while | flops 42631688 | bytes 537676 | solution.py:71
  87.8 1.9 fusion.100
  95.7 103.4 %while.53 = (s32[]{:T(128)}, f32[8,128,128]{2,1,0:T(8,128)}, f32[8,128,128]{2,1,0:T(8,128)}, f32[8]{0:T(128)S(1)}, f32[8,128,128]{2,1,0:T(8,128)S(1)}, /*index=5*/s32[]{:T(128)}) while((s32[]{:T(128)}, f32[8,128,128]{2,1,0:T(8,128)}, f32[8,128,128]{2,1,0:T(8,128)}, f32[8]{0:T(128)S(1)}, f32[8,128,128]{2,1,0:T(8,128)S(1)}, ...), condition=%wide.region_8.9_spmd, body=%wide.region_7.8_spmd.sunk | while | flops 262146 | bytes 5767337 | solution.py:80
  95.7 4.9 %collective-permute-start = (f32[8,128,128]{2,1,0:T(8,128)}, f32[8,128,128]{2,1,0:T(8,128)S(1)}, u32[]{:S(2)}, u32[]{:S(2)}) collective-permute-start(f32[8,128,128]{2,1,0:T(8,128)} %get-tuple-element.685), channel_id=1, source_target_pairs={{0,1},{1,2},{2,3},{3,4},{4,5},{5,6},{6,7},{8,9},{9,10},{10,11},{11... | collective-permute-start | bytes 1572872 | tf_op jit(solution)/shard_map/while/body/eval_jaxpr/ppermute | solution.py:12
  100.6 11.4 %collective-permute-done = f32[8,128,128]{2,1,0:T(8,128)S(1)} collective-permute-done((f32[8,128,128]{2,1,0:T(8,128)}, f32[8,128,128]{2,1,0:T(8,128)S(1)}, u32[]{:S(2)}, u32[]{:S(2)}) %collective-permute-start) | collective-permute-done | bytes 524320 | tf_op jit(solution)/shard_map/while/body/eval_jaxpr/ppermute | solution.py:12
  113.0 4.3 %collective-permute-start = (f32[8,128,128]{2,1,0:T(8,128)}, f32[8,128,128]{2,1,0:T(8,128)S(1)}, u32[]{:S(2)}, u32[]{:S(2)}) collective-permute-start(f32[8,128,128]{2,1,0:T(8,128)} %get-tuple-element.685), channel_id=1, source_target_pairs={{0,1},{1,2},{2,3},{3,4},{4,5},{5,6},{6,7},{8,9},{9,10},{10,11},{11... | collective-permute-start | bytes 1572872 | tf_op jit(solution)/shard_map/while/body/eval_jaxpr/ppermute | solution.py:12
  117.3 10.6 %collective-permute-done = f32[8,128,128]{2,1,0:T(8,128)S(1)} collective-permute-done((f32[8,128,128]{2,1,0:T(8,128)}, f32[8,128,128]{2,1,0:T(8,128)S(1)}, u32[]{:S(2)}, u32[]{:S(2)}) %collective-permute-start) | collective-permute-done | bytes 524320 | tf_op jit(solution)/shard_map/while/body/eval_jaxpr/ppermute | solution.py:12
  128.9 4.3 %collective-permute-start = (f32[8,128,128]{2,1,0:T(8,128)}, f32[8,128,128]{2,1,0:T(8,128)S(1)}, u32[]{:S(2)}, u32[]{:S(2)}) collective-permute-start(f32[8,128,128]{2,1,0:T(8,128)} %get-tuple-element.685), channel_id=1, source_target_pairs={{0,1},{1,2},{2,3},{3,4},{4,5},{5,6},{6,7},{8,9},{9,10},{10,11},{11... | collective-permute-start | bytes 1572872 | tf_op jit(solution)/shard_map/while/body/eval_jaxpr/ppermute | solution.py:12
  133.3 9.7 %collective-permute-done = f32[8,128,128]{2,1,0:T(8,128)S(1)} collective-permute-done((f32[8,128,128]{2,1,0:T(8,128)}, f32[8,128,128]{2,1,0:T(8,128)S(1)}, u32[]{:S(2)}, u32[]{:S(2)}) %collective-permute-start) | collective-permute-done | bytes 524320 | tf_op jit(solution)/shard_map/while/body/eval_jaxpr/ppermute | solution.py:12
  143.9 5.2 %collective-permute-start = (f32[8,128,128]{2,1,0:T(8,128)}, f32[8,128,128]{2,1,0:T(8,128)S(1)}, u32[]{:S(2)}, u32[]{:S(2)}) collective-permute-start(f32[8,128,128]{2,1,0:T(8,128)} %get-tuple-element.685), channel_id=1, source_target_pairs={{0,1},{1,2},{2,3},{3,4},{4,5},{5,6},{6,7},{8,9},{9,10},{10,11},{11... | collective-permute-start | bytes 1572872 | tf_op jit(solution)/shard_map/while/body/eval_jaxpr/ppermute | solution.py:12
  149.1 8.7 %collective-permute-done = f32[8,128,128]{2,1,0:T(8,128)S(1)} collective-permute-done((f32[8,128,128]{2,1,0:T(8,128)}, f32[8,128,128]{2,1,0:T(8,128)S(1)}, u32[]{:S(2)}, u32[]{:S(2)}) %collective-permute-start) | collective-permute-done | bytes 524320 | tf_op jit(solution)/shard_map/while/body/eval_jaxpr/ppermute | solution.py:12
  158.8 5.2 %collective-permute-start = (f32[8,128,128]{2,1,0:T(8,128)}, f32[8,128,128]{2,1,0:T(8,128)S(1)}, u32[]{:S(2)}, u32[]{:S(2)}) collective-permute-start(f32[8,128,128]{2,1,0:T(8,128)} %get-tuple-element.685), channel_id=1, source_target_pairs={{0,1},{1,2},{2,3},{3,4},{4,5},{5,6},{6,7},{8,9},{9,10},{10,11},{11... | collective-permute-start | bytes 1572872 | tf_op jit(solution)/shard_map/while/body/eval_jaxpr/ppermute | solution.py:12
  164.0 7.8 %collective-permute-done = f32[8,128,128]{2,1,0:T(8,128)S(1)} collective-permute-done((f32[8,128,128]{2,1,0:T(8,128)}, f32[8,128,128]{2,1,0:T(8,128)S(1)}, u32[]{:S(2)}, u32[]{:S(2)}) %collective-permute-start) | collective-permute-done | bytes 524320 | tf_op jit(solution)/shard_map/while/body/eval_jaxpr/ppermute | solution.py:12
  172.8 5.2 %collective-permute-start = (f32[8,128,128]{2,1,0:T(8,128)}, f32[8,128,128]{2,1,0:T(8,128)S(1)}, u32[]{:S(2)}, u32[]{:S(2)}) collective-permute-start(f32[8,128,128]{2,1,0:T(8,128)} %get-tuple-element.685), channel_id=1, source_target_pairs={{0,1},{1,2},{2,3},{3,4},{4,5},{5,6},{6,7},{8,9},{9,10},{10,11},{11... | collective-permute-start | bytes 1572872 | tf_op jit(solution)/shard_map/while/body/eval_jaxpr/ppermute | solution.py:12
  178.0 7.0 %collective-permute-done = f32[8,128,128]{2,1,0:T(8,128)S(1)} collective-permute-done((f32[8,128,128]{2,1,0:T(8,128)}, f32[8,128,128]{2,1,0:T(8,128)S(1)}, u32[]{:S(2)}, u32[]{:S(2)}) %collective-permute-start) | collective-permute-done | bytes 524320 | tf_op jit(solution)/shard_map/while/body/eval_jaxpr/ppermute | solution.py:12
  186.0 5.2 %collective-permute-start = (f32[8,128,128]{2,1,0:T(8,128)}, f32[8,128,128]{2,1,0:T(8,128)S(1)}, u32[]{:S(2)}, u32[]{:S(2)}) collective-permute-start(f32[8,128,128]{2,1,0:T(8,128)} %get-tuple-element.685), channel_id=1, source_target_pairs={{0,1},{1,2},{2,3},{3,4},{4,5},{5,6},{6,7},{8,9},{9,10},{10,11},{11... | collective-permute-start | bytes 1572872 | tf_op jit(solution)/shard_map/while/body/eval_jaxpr/ppermute | solution.py:12
  191.2 7.0 %collective-permute-done = f32[8,128,128]{2,1,0:T(8,128)S(1)} collective-permute-done((f32[8,128,128]{2,1,0:T(8,128)}, f32[8,128,128]{2,1,0:T(8,128)S(1)}, u32[]{:S(2)}, u32[]{:S(2)}) %collective-permute-start) | collective-permute-done | bytes 524320 | tf_op jit(solution)/shard_map/while/body/eval_jaxpr/ppermute | solution.py:12
  199.1 55.8 %while.54 = (s32[]{:T(128)}, bf16[8,256,128]{1,2,0:T(8,128)(2,1)}, f32[8,256,128]{2,1,0:T(8,128)}, s32[8]{0:T(128)S(1)}, bf16[256,1024]{1,0:T(8,128)(2,1)}, /*in...) while((s32[]{:T(128)}, bf16[8,256,128]{1,2,0:T(8,128)(2,1)}, ...), condition=%wide.region_12.13_spmd, body=%wide.region_9.12_spmd.sunk | while | flops 25526792 | bytes 1328113 | solution.py:97
  254.9 41.3 %while.56 = (s32[]{:T(128)}, f32[8,2,512]{2,1,0:T(2,128)S(1)}, f32[8,2,512]{2,1,0:T(2,128)S(1)}, f32[8,2,512]{2,1,0:T(2,128)S(1)}, s32[8]{0:T(128)S(1)}, /*index...) while((s32[]{:T(128)}, f32[8,2,512]{2,1,0:T(2,128)S(1)}, ...), condition=%wide.region_16.17_spmd.clone.clone, body=%wide.region_13.16_spmd.clone.clone.sunk | while | flops 74843648 | bytes 5143243 | solution.py:122
  296.2 38.5 %pmax.7 = f32[8,2,512]{2,1,0:T(2,128)S(1)} all-reduce(f32[8,2,512]{2,1,0:T(2,128)S(1)} %get-tuple-element.206), channel_id=1, replica_groups=mesh['dp'=4,'ctx'=8] {'ctx'}, use_global_device_ids=true, to_apply=%region_17.18 | all-reduce | flops 8192 | bytes 65536 | tf_op jit(solution)/shard_map/pmax | solution.py:127
  336.2 2.0 copy.26
  338.3 64.6 %all-reduce.3.cloned.1.call-done = (f32[8,2,512]{2,1,0:T(2,128)}, f32[8,2,512]{2,1,0:T(2,128)}, f32[2,512]{1,0:T(2,128)}) async-done(((f32[8,2,512]{2,1,0:T(2,128)}, f32[8,2,512]{2,1,0:T(2,128)}, f32[2,512]{1,0:T(2,128)}), (f32[8,2,512]{2,1,0:T(2,128)}, f32[8,2,512]{2,1,0:T(2,128)}, f32[2,512]{1,0:T(2,128)})) %all-reduce.3.cloned.1.call-update) | async-done | bytes 69648 | tf_op jit(solution)/shard_map/psum | solution.py:129
  405.7 6.3 %psum.31 = f32[]{:T(128)} all-reduce(f32[]{:T(128)} %get-tuple-element.395), channel_id=1, replica_groups=mesh['dp'=4,'ctx'=8] {'dp'}, use_global_device_ids=true, to_apply=%region_24.25 | all-reduce | flops 1 | bytes 8 | tf_op jit(solution)/shard_map/psum | solution.py:135
  (293 shorter events, 134.4 us)
Async XLA Ops:
  7.2 5.9 %copy-start = (bf16[1024,1024]{1,0:T(8,128)(2,1)S(1)}, bf16[1024,1024]{1,0:T(8,128)(2,1)}, u32[]{:S(2)}) copy-start(bf16[1024,1024]{1,0:T(8,128)(2,1)} %param.22) | copy-start | bytes 6291460
  7.2 8.6 %copy-start.2 = (bf16[1,256,1024]{2,1,0:T(8,128)(2,1)S(1)}, bf16[1,256,1024]{2,1,0:T(8,128)(2,1)}, u32[]{:S(2)}) copy-start(bf16[1,256,1024]{2,1,0:T(8,128)(2,1)} %param.18) | copy-start | bytes 1572868
  7.2 395.7 %all-reduce.3.cloned.1.call-start = ((), (), s32[]{:S(2)}) async-start(), calls=%async_computation | async-start | bytes 139264 | tf_op jit(solution)/shard_map/psum | solution.py:129
  13.0 2.8 copy-start.5
  15.8 1.6 copy-start.6
  95.7 16.3 %collective-permute-start = (f32[8,128,128]{2,1,0:T(8,128)}, f32[8,128,128]{2,1,0:T(8,128)S(1)}, u32[]{:S(2)}, u32[]{:S(2)}) collective-permute-start(f32[8,128,128]{2,1,0:T(8,128)} %get-tuple-element.685), channel_id=1, source_target_pairs={{0,1},{1,2},{2,3},{3,4},{4,5},{5,6},{6,7},{8,9},{9,10},{10,11},{11... | collective-permute-start | bytes 1572872 | tf_op jit(solution)/shard_map/while/body/eval_jaxpr/ppermute | solution.py:12
  112.0 1.0 copy-start.1
  113.0 14.9 %collective-permute-start = (f32[8,128,128]{2,1,0:T(8,128)}, f32[8,128,128]{2,1,0:T(8,128)S(1)}, u32[]{:S(2)}, u32[]{:S(2)}) collective-permute-start(f32[8,128,128]{2,1,0:T(8,128)} %get-tuple-element.685), channel_id=1, source_target_pairs={{0,1},{1,2},{2,3},{3,4},{4,5},{5,6},{6,7},{8,9},{9,10},{10,11},{11... | collective-permute-start | bytes 1572872 | tf_op jit(solution)/shard_map/while/body/eval_jaxpr/ppermute | solution.py:12
  127.9 1.0 copy-start.1
  128.9 14.0 %collective-permute-start = (f32[8,128,128]{2,1,0:T(8,128)}, f32[8,128,128]{2,1,0:T(8,128)S(1)}, u32[]{:S(2)}, u32[]{:S(2)}) collective-permute-start(f32[8,128,128]{2,1,0:T(8,128)} %get-tuple-element.685), channel_id=1, source_target_pairs={{0,1},{1,2},{2,3},{3,4},{4,5},{5,6},{6,7},{8,9},{9,10},{10,11},{11... | collective-permute-start | bytes 1572872 | tf_op jit(solution)/shard_map/while/body/eval_jaxpr/ppermute | solution.py:12
  142.9 1.0 copy-start.1
  143.9 13.9 %collective-permute-start = (f32[8,128,128]{2,1,0:T(8,128)}, f32[8,128,128]{2,1,0:T(8,128)S(1)}, u32[]{:S(2)}, u32[]{:S(2)}) collective-permute-start(f32[8,128,128]{2,1,0:T(8,128)} %get-tuple-element.685), channel_id=1, source_target_pairs={{0,1},{1,2},{2,3},{3,4},{4,5},{5,6},{6,7},{8,9},{9,10},{10,11},{11... | collective-permute-start | bytes 1572872 | tf_op jit(solution)/shard_map/while/body/eval_jaxpr/ppermute | solution.py:12
  157.8 1.0 copy-start.1
  158.8 13.0 %collective-permute-start = (f32[8,128,128]{2,1,0:T(8,128)}, f32[8,128,128]{2,1,0:T(8,128)S(1)}, u32[]{:S(2)}, u32[]{:S(2)}) collective-permute-start(f32[8,128,128]{2,1,0:T(8,128)} %get-tuple-element.685), channel_id=1, source_target_pairs={{0,1},{1,2},{2,3},{3,4},{4,5},{5,6},{6,7},{8,9},{9,10},{10,11},{11... | collective-permute-start | bytes 1572872 | tf_op jit(solution)/shard_map/while/body/eval_jaxpr/ppermute | solution.py:12
  171.8 1.0 copy-start.1
  172.8 12.2 %collective-permute-start = (f32[8,128,128]{2,1,0:T(8,128)}, f32[8,128,128]{2,1,0:T(8,128)S(1)}, u32[]{:S(2)}, u32[]{:S(2)}) collective-permute-start(f32[8,128,128]{2,1,0:T(8,128)} %get-tuple-element.685), channel_id=1, source_target_pairs={{0,1},{1,2},{2,3},{3,4},{4,5},{5,6},{6,7},{8,9},{9,10},{10,11},{11... | collective-permute-start | bytes 1572872 | tf_op jit(solution)/shard_map/while/body/eval_jaxpr/ppermute | solution.py:12
  185.0 1.0 copy-start.1
  186.0 12.2 %collective-permute-start = (f32[8,128,128]{2,1,0:T(8,128)}, f32[8,128,128]{2,1,0:T(8,128)S(1)}, u32[]{:S(2)}, u32[]{:S(2)}) collective-permute-start(f32[8,128,128]{2,1,0:T(8,128)} %get-tuple-element.685), channel_id=1, source_target_pairs={{0,1},{1,2},{2,3},{3,4},{4,5},{5,6},{6,7},{8,9},{9,10},{10,11},{11... | collective-permute-start | bytes 1572872 | tf_op jit(solution)/shard_map/while/body/eval_jaxpr/ppermute | solution.py:12
  198.2 1.0 copy-start.1
  254.9 79.8 %copy-start.7 = (s32[1,256]{1,0:T(1,128)S(1)}, s32[1,256]{1,0:T(1,128)}, u32[]{:S(2)}) copy-start(s32[1,256]{1,0:T(1,128)} %param.21) | copy-start | bytes 3076
  254.9 81.3 %copy-start.4 = (s32[1,2]{1,0:T(1,128)S(1)}, s32[1,2]{1,0:T(1,128)}, u32[]{:S(2)}) copy-start(s32[1,2]{1,0:T(1,128)} %param.20) | copy-start | bytes 28
  403.7 8.9 %copy-start.3 = (f32[2,512]{1,0:T(2,128)}, f32[2,512]{1,0:T(2,128)S(1)}, u32[]{:S(2)}) copy-start(f32[2,512]{1,0:T(2,128)S(1)} %divide_reduce_fusion) | copy-start | bytes 12292
Sparse Core Ops, SparseCore 0:
  336.3 66.5 all-reduce.2
where the time goes:
time: 424 us; the launch traced here: 421 us
  waiting for transfers between devices  127 us (30%)
  matrix products  66.8 us (16%)
  loops' own time  57.1 us (13%)
  blocking collectives  44.8 us (11%)
  local copies, waits for them, and re-layouts  44.4 us (10%)
  starting transfers between devices  34.4 us (8%)
  other arithmetic  29.7 us (7%)
  between operations  16.6 us (4%)
    psum x1, waiting for transfers between devices, local(): lax.psum((mass_part * rescale, weighted * rescale, counts), 'ctx')  64.6 us
    ppermute x7, waiting for transfers between devices, passed_along(): return lax.ppermute(x, axis, pairs)  62.2 us
    pmax x1, blocking collectives, local(): top_score = lax.pmax(maxima, 'ctx')  38.5 us
    ppermute x7, starting transfers between devices, passed_along(): return lax.ppermute(x, axis, pairs)  34.3 us
    another operation x1, loops' own time, local(): lax.map(local_head, jnp.arange(head_count, dtype=jnp.int32))  30.3 us
    another operation x1, loops' own time, local(): lax.map(finish_head, (jnp.arange(head_count, dtype=jnp.int32), intra_all,...  21.1 us
    dot_general x8, matrix products, local_head(): intra_sum = jnp.dot(weights, v_head, preferred_element_type=jnp.float32)  15 us
    dynamic_slice x24, local copies, waits for them, and re-layouts, local(): lax.map(local_head, jnp.arange(head_count, dtype=jnp.int32))  14.2 us
  transfers between devices with their start and end apart: 8, of which 8 were waited for; matrix products, arithmetic and copies ran while one was open for 0% of the time, Pallas kernels for 0%

commit v1 on v0

v1 whole, which is shorter than its diff:
```python
import functools
import math

import jax
import jax.numpy as jnp
from jax import lax
from jax.experimental import pallas as pl
from jax.experimental.pallas import tpu as pltpu
from jax.sharding import PartitionSpec as P

NEG_FILL = -1e30
LOG2E = math.log2(math.e)
F32 = jnp.float32
BF16 = jnp.bfloat16
NT = (((1,), (1,)), ((), ()))
TN = (((0,), (0,)), ((), ()))
PAD = 8


def fused(
    n,
    dp_n,
    lengths_ref,
    decay_ref,
    label_ref,
    gain_ref,
    tokens_hbm,
    wq_hbm,
    wk_hbm,
    wv_hbm,
    lq_hbm,
    lw_hbm,
    out_hbm,
    logits_ref,
    loss_ref,
    mean_ref,
    x_ref,
    wq_ref,
    wk_ref,
    wv_ref,
    lq_ref,
    lw_ref,
    q_ref,
    k_ref,
    v_ref,
    ccol,
    crow,
    pair_bias,
    intra,
    pool_w,
    weighted,
    out_buf,
    loc,
    peer_loc,
    chain_in,
    chain_out,
    hand,
    state,
    stats,
    stat_in,
    lse,
    contrib,
    contrib_in,
    loss_out,
    loss_in,
    in_sem,
    out_sem,
    loc_send,
    loc_recv,
    chain_send,
    chain_recv,
    hand_send,
    hand_recv,
    stat_send,
    stat_recv,
    lse_send,
    lse_recv,
    con_send,
    con_recv,
    dp_send,
    dp_recv,
):
    tok, width = x_ref.shape
    heads, _, hd = q_ref.shape
    labels = lq_ref.shape[0]
    recs = lengths_ref.shape[1]
    half_heads = heads // 2
    pairs = n // 2
    scale = hd ** (-0.5)
    soft = scale * LOG2E
    me = lax.axis_index("ctx")
    my_dp = lax.axis_index("dp")
    half = lax.rem(me, 2)
    pair = me // 2
    partner = me + 1 - 2 * half
    even = half == 0

    loads = [
        pltpu.make_async_copy(src, dst, in_sem.at[i])
        for i, (src, dst) in enumerate(
            (
                (tokens_hbm, x_ref),
                (wk_hbm, wk_ref),
                (wv_hbm, wv_ref),
                (wq_hbm, wq_ref),
                (lq_hbm, lq_ref),
                (lw_hbm, lw_ref),
            )
        )
    ]
    for load in loads:
        load.start()

    barrier = pltpu.get_barrier_semaphore()
    for d in range(1, n):
        pl.semaphore_signal(
            barrier,
            inc=1,
            device_id={"ctx": lax.rem(me + d, n)},
            device_id_type=pl.DeviceIdType.MESH,
        )
    for d in range(1, dp_n):
        pl.semaphore_signal(
            barrier,
            inc=1,
            device_id={"dp": lax.rem(my_dp + d, dp_n)},
            device_id_type=pl.DeviceIdType.MESH,
        )

    def send(src, dst, ssem, rsem, where):
        return pltpu.make_async_remote_copy(
            src_ref=src,
            dst_ref=dst,
            send_sem=ssem,
            recv_sem=rsem,
            device_id=where,
            device_id_type=pl.DeviceIdType.MESH,
        )

    shard_start = me * tok
    starts = []
    run = jnp.int32(0)
    for r in range(recs):
        starts.append(run)
        run = run + lengths_ref[0, r]

    def record_of(pos):
        rec = jnp.full_like(pos, -1)
        for r in range(recs):
            rec = rec + (starts[r] <= pos).astype(jnp.int32)
        return rec

    def record_scalar(pos):
        rec = jnp.int32(-1)
        for r in range(recs):
            rec = rec + (starts[r] <= pos).astype(jnp.int32)
        return rec

    before_rec = record_scalar(shard_start - 1)
    last_rec = record_scalar(shard_start + tok - 1)

    def col_record(lanes):
        return record_of(shard_start + lax.broadcasted_iota(jnp.int32, (tok, lanes), 0))

    def row_record(rows):
        return record_of(shard_start + lax.broadcasted_iota(jnp.int32, (rows, tok), 1))

    down = lax.broadcasted_iota(jnp.int32, (tok, tok), 0)
    across = lax.broadcasted_iota(jnp.int32, (tok, tok), 1)
    tri_low = (across <= down).astype(F32)
    decays = decay_ref[...]
    cum_rows = (
        lax.dot_general(
            decays, tri_low, NT, precision=lax.Precision.HIGHEST, preferred_element_type=F32
        )
        * LOG2E
    )
    cum_cols = (
        lax.dot_general(
            tri_low, decays, NT, precision=lax.Precision.HIGHEST, preferred_element_type=F32
        )
        * LOG2E
    )
    for h in range(heads):
        crow[h] = cum_rows[h : h + 1, :]
        ccol[h] = jnp.broadcast_to(cum_cols[:, h : h + 1], (tok, hd))
    pair_ok = (across <= down) & (col_record(tok) == row_record(tok))
    pair_bias[...] = jnp.where(pair_ok, math.log2(scale), NEG_FILL)

    def project(w_ref, dst):
        step = min(256, width)
        for c in range(width // step):
            res = jnp.dot(
                x_ref[...], w_ref[:, c * step : (c + 1) * step], preferred_element_type=F32
            ).astype(BF16)
            for s in range(step // hd):
                dst[c * (step // hd) + s] = res[:, s * hd : (s + 1) * hd]

    loads[0].wait()
    loads[1].wait()
    project(wk_ref, k_ref)
    loads[2].wait()
    project(wv_ref, v_ref)

    def local_state(h):
        cum = ccol[h]
        last = cum[tok - 1 : tok, :]
        fade = jnp.exp2(jnp.where(col_record(hd) == last_rec, last - cum, NEG_FILL))
        kdec = (k_ref[h].astype(F32) * fade).astype(BF16)
        loc[h, :hd, :] = lax.dot_general(kdec, v_ref[h], TN, preferred_element_type=F32)
        carry = jnp.where(last_rec == before_rec, jnp.exp2(last), 0.0)
        loc[h, hd:, :] = jnp.broadcast_to(carry, (PAD, hd))

    def loc_copy(i):
        h = (1 - half) * half_heads + i
        return send(
            loc.at[h], peer_loc.at[i], loc_send.at[i], loc_recv.at[i], {"ctx": partner}
        )

    pl.semaphore_wait(barrier, n - 1 + dp_n - 1)

    @pl.when(pair == 0)
    def _():
        chain_in[...] = jnp.zeros_like(chain_in)

    for i in range(half_heads):
        local_state((1 - half) * half_heads + i)
        loc_copy(i).start()
    for i in range(half_heads):
        local_state(half * half_heads + i)

    def chain_copy(i):
        return send(
            chain_out.at[i],
            chain_in.at[i],
            chain_send.at[i],
            chain_recv.at[i],
            {"ctx": lax.rem(me + 2, n)},
        )

    def hand_copy(i):
        return send(
            hand.at[i],
            state.at[half * half_heads + i],
            hand_send.at[i],
            hand_recv.at[i],
            {"ctx": partner},
        )

    def hand_arrival(i):
        return send(
            hand.at[i],
            state.at[(1 - half) * half_heads + i],
            hand_send.at[i],
            hand_recv.at[i],
            {"ctx": partner},
        )

    def chain_step(i):
        h = half * half_heads + i
        loc_copy(i).wait_recv()

        @pl.when(pair > 0)
        def _():
            chain_copy(i).wait_recv()

        came = chain_in[i]
        own = loc[h]
        other = peer_loc[i]
        first = jnp.where(even, own, other)
        second = jnp.where(even, other, own)
        middle = first[hd : hd + 1, :] * came + first[:hd, :]

        @pl.when(pair < pairs - 1)
        def _():
            chain_out[i] = second[hd : hd + 1, :] * middle + second[:hd, :]
            chain_copy(i).start()

        hand[i] = jnp.where(even, middle, came)
        hand_copy(i).start()
        state[h] = jnp.where(even, came, middle)

    units = 2 * heads
    first_unit = jnp.minimum(1 + 3 * pair, units - half_heads)

    def maybe_chain(unit):
        i = unit - first_unit

        @pl.when((i >= 0) & (i < half_heads))
        def _():
            chain_step(i)

    loads[3].wait()
    project(wq_ref, q_ref)
    loads[4].wait()

    chunk = min(256, labels)

    def pool_unit(h):
        lanes = pl.ds(pl.multiple_of(h * hd, hd), hd)
        rec = col_record(chunk)
        for c in range(labels // chunk):
            cols = slice(c * chunk, (c + 1) * chunk)
            scores = lax.dot_general(
                x_ref[:, lanes], lq_ref[cols, lanes], NT, preferred_element_type=F32
            )
            tops = [
                jnp.max(jnp.where(rec == r, scores, NEG_FILL), axis=0, keepdims=True)
                for r in range(recs)
            ]
            top = tops[0]
            for r in range(1, recs):
                top = jnp.where(rec == r, tops[r], top)
            weight = jnp.exp2((scores - top) * soft)
            pool_w[h, :, cols] = weight
            for r in range(recs):
                stats[h, r : r + 1, cols] = tops[r] * soft
                stats[h, recs + r : recs + r + 1, cols] = jnp.sum(
                    jnp.where(rec == r, weight, 0.0), axis=0, keepdims=True
                )

    def pool_body(h, _):
        pool_unit(h)
        maybe_chain(h)
        return 0

    lax.fori_loop(0, heads, pool_body, 0)

    def stat_copy(d):
        target = lax.rem(me + d, n)
        return target, send(
            stats.at[lax.rem(target, heads)],
            stat_in.at[me],
            stat_send.at[d],
            stat_recv.at[d],
            {"ctx": target},
        )

    def stat_arrival(d):
        return send(
            stats.at[0],
            stat_in.at[lax.rem(me - d + n, n)],
            stat_send.at[d],
            stat_recv.at[d],
            {"ctx": lax.rem(me + d, n)},
        )

    def each_peer(fn):
        for d in range(1, n):
            fn(d)

    def start_stat(d):
        target, copy = stat_copy(d)

        @pl.when(target < heads)
        def _():
            copy.start()

    each_peer(start_stat)

    def intra_unit(h):
        scores = lax.dot_general(q_ref[h], k_ref[h], NT, preferred_element_type=F32)
        cum = jnp.concatenate([ccol[h]] * (tok // hd), axis=1)
        fade = jnp.exp2(cum - crow[h] + pair_bias[...])
        weights = (scores * fade).astype(BF16)
        intra[h] = jnp.dot(weights, v_ref[h], preferred_element_type=F32)

    def intra_body(h, _):
        intra_unit(h)
        maybe_chain(heads + h)
        return 0

    lax.fori_loop(0, heads, intra_body, 0)

    def lse_copy(d):
        return send(
            lse.at[lax.rem(me, heads)],
            lse.at[lax.rem(me, heads)],
            lse_send.at[d],
            lse_recv.at[d],
            {"ctx": lax.rem(me + d, n)},
        )

    def lse_arrival(d):
        source = lax.rem(me - d + n, n)
        return source, send(
            lse.at[lax.rem(source, heads)],
            lse.at[lax.rem(source, heads)],
            lse_send.at[d],
            lse_recv.at[d],
            {"ctx": lax.rem(me + d, n)},
        )

    @pl.when(me < heads)
    def _():
        stat_in[me] = stats[lax.rem(me, heads)]
        each_peer(lambda d: stat_arrival(d).wait_recv())
        top = stat_in[0, :recs, :]
        for j in range(1, n):
            top = jnp.maximum(top, stat_in[j, :recs, :])
        mass = jnp.zeros_like(top)
        for j in range(n):
            mass = mass + stat_in[j, recs:, :] * jnp.exp2(stat_in[j, :recs, :] - top)
        lse[lax.rem(me, heads)] = top + jnp.log(mass) * LOG2E
        each_peer(lambda d: lse_copy(d).start())

    hot = (
        lax.broadcasted_iota(jnp.int32, (labels, tok), 0) == label_ref[...]
    ).astype(F32).astype(BF16)
    members = (
        row_record(16) == lax.broadcasted_iota(jnp.int32, (16, tok), 0)
    ).astype(F32).astype(BF16)
    counts = lax.dot_general(members, hot, NT, preferred_element_type=F32)
    contrib[recs:, :] = counts[:recs, :]

    loads[5].wait()

    def finish(h):
        lanes = pl.ds(pl.multiple_of(h * hd, hd), hd)
        st = state[h]
        high = st.astype(BF16)
        low = (st - high.astype(F32)).astype(BF16)
        q = q_ref[h]
        inter = jnp.dot(
            jnp.concatenate([q, q], axis=1),
            jnp.concatenate([high, low], axis=0),
            preferred_element_type=F32,
        )
        fade = jnp.exp2(
            jnp.where(col_record(hd) == before_rec, ccol[h] + math.log2(scale), NEG_FILL)
        )
        total = intra[h] + inter * fade
        centred = total - jnp.mean(total, axis=1, keepdims=True)
        variance = jnp.mean(centred * centred, axis=1, keepdims=True)
        rows = (centred * lax.rsqrt(variance + 1e-05) * gain_ref[pl.ds(h, 1), :]).astype(BF16)
        out_buf[:, lanes] = rows
        rec = col_record(chunk)
        for c in range(labels // chunk):
            cols = slice(c * chunk, (c + 1) * chunk)
            value = lax.dot_general(rows, lw_ref[cols, lanes], NT, preferred_element_type=F32)
            value = value * pool_w[h, :, cols]
            for r in range(recs):
                weighted[h, r : r + 1, cols] = jnp.sum(
                    jnp.where(rec == r, value, 0.0), axis=0, keepdims=True
                )

    def finish_own(i, _):
        finish(half * half_heads + i)
        return 0

    def finish_other(i, _):
        hand_arrival(i).wait_recv()
        finish((1 - half) * half_heads + i)
        return 0

    lax.fori_loop(0, half_heads, finish_own, 0)
    lax.fori_loop(0, half_heads, finish_other, 0)

    store = pltpu.make_async_copy(out_buf, out_hbm, out_sem)
    store.start()

    def wait_lse(d):
        source, copy = lse_arrival(d)

        @pl.when(source < heads)
        def _():
            copy.wait_recv()

    each_peer(wait_lse)
    part = jnp.zeros((recs, labels), F32)
    for h in range(heads):
        part = part + weighted[h] * jnp.exp2(stats[h, :recs, :] - lse[h])
    contrib[:recs, :] = part

    def con_copy(d):
        return send(
            contrib,
            contrib_in.at[d],
            con_send.at[d],
            con_recv.at[d],
            {"ctx": lax.rem(me + d, n)},
        )

    each_peer(lambda d: con_copy(d).start())
    contrib_in[0] = contrib[...]
    each_peer(lambda d: con_copy(d).wait_recv())
    both = contrib_in[lax.rem(me, n)]
    for j in range(1, n):
        both = both + contrib_in[lax.rem(me - j + n, n)]
    logits = both[:recs, :]
    logits_ref[...] = logits
    losses = []
    total_loss = jnp.zeros((1, 1), F32)
    for r in range(recs):
        z = logits[r : r + 1, :]
        target = (both[recs + r : recs + r + 1, :] + 0.5) / (
            lengths_ref[0, r].astype(F32) + 1.0
        )
        soft_plus = jnp.maximum(z, 0.0) + jnp.log1p(jnp.exp(-jnp.abs(z)))
        value = jnp.mean(soft_plus - target * z, axis=1, keepdims=True)
        losses.append(value)
        total_loss = total_loss + value
    spot = lax.broadcasted_iota(jnp.int32, (1, recs), 1)
    row = jnp.zeros((1, recs), F32)
    for r in range(recs):
        row = jnp.where(spot == r, losses[r], row)
    loss_ref[...] = row
    loss_out[...] = jnp.broadcast_to(total_loss, loss_out.shape)

    def dp_copy(d):
        return send(
            loss_out,
            loss_in.at[d],
            dp_send.at[d],
            dp_recv.at[d],
            {"dp": lax.rem(my_dp + d, dp_n)},
        )

    for d in range(1, dp_n):
        dp_copy(d).start()
    loss_in[0] = loss_out[...]
    for d in range(1, dp_n):
        dp_copy(d).wait_recv()
    total = loss_in[lax.rem(my_dp, dp_n)]
    for j in range(1, dp_n):
        total = total + loss_in[lax.rem(my_dp - j + dp_n, dp_n)]
    mean_ref[...] = total[:1, :1] / (dp_n * recs)

    for d in range(1, dp_n):
        dp_copy(d).wait_send()
    each_peer(lambda d: con_copy(d).wait_send())

    @pl.when(me < heads)
    def _():
        each_peer(lambda d: lse_copy(d).wait_send())

    def end_stat(d):
        target, copy = stat_copy(d)

        @pl.when(target < heads)
        def _():
            copy.wait_send()

    each_peer(end_stat)
    for i in range(half_heads):
        loc_copy(i).wait_send()
        hand_copy(i).wait_send()

    @pl.when(pair < pairs - 1)
    def _():
        for i in range(half_heads):
            chain_copy(i).wait_send()

    store.wait()


def local(
    tokens,
    log_decay,
    lengths,
    label_ids,
    w_query,
    w_key,
    w_value,
    norm_gain,
    label_query,
    label_weight,
):
    n = lax.axis_size("ctx")
    dp_n = lax.axis_size("dp")
    tok, width = tokens.shape[1:]
    heads = log_decay.shape[1]
    hd = width // heads
    recs = lengths.shape[1]
    labels = label_query.shape[0]
    half = heads // 2
    assert n >= heads and n % 2 == 0
    any_space = pl.BlockSpec(memory_space=pl.ANY)
    vmem = pl.BlockSpec(memory_space=pltpu.VMEM)
    smem = pl.BlockSpec(memory_space=pltpu.SMEM)
    dma = pltpu.SemaphoreType.DMA
    out, logits, loss, mean = pl.pallas_call(
        functools.partial(fused, n, dp_n),
        out_shape=(
            jax.ShapeDtypeStruct((tok, width), BF16),
            jax.ShapeDtypeStruct((recs, labels), F32),
            jax.ShapeDtypeStruct((1, recs), F32),
            jax.ShapeDtypeStruct((1, 1), F32),
        ),
        in_specs=[smem, vmem, vmem, vmem] + [any_space] * 6,
        out_specs=(any_space, vmem, vmem, vmem),
        scratch_shapes=[
            pltpu.VMEM((tok, width), BF16),
            pltpu.VMEM((width, width), BF16),
            pltpu.VMEM((width, width), BF16),
            pltpu.VMEM((width, width), BF16),
            pltpu.VMEM((labels, width), BF16),
            pltpu.VMEM((labels, width), BF16),
            pltpu.VMEM((heads, tok, hd), BF16),
            pltpu.VMEM((heads, tok, hd), BF16),
            pltpu.VMEM((heads, tok, hd), BF16),
            pltpu.VMEM((heads, tok, hd), F32),
            pltpu.VMEM((heads, 1, tok), F32),
            pltpu.VMEM((tok, tok), F32),
            pltpu.VMEM((heads, tok, hd), F32),
            pltpu.VMEM((heads, tok, labels), F32),
            pltpu.VMEM((heads, recs, labels), F32),
            pltpu.VMEM((tok, width), BF16),
            pltpu.VMEM((heads, hd + PAD, hd), F32),
            pltpu.VMEM((half, hd + PAD, hd), F32),
            pltpu.VMEM((half, hd, hd), F32),
            pltpu.VMEM((half, hd, hd), F32),
            pltpu.VMEM((half, hd, hd), F32),
            pltpu.VMEM((heads, hd, hd), F32),
            pltpu.VMEM((heads, 2 * recs, labels), F32),
            pltpu.VMEM((n, 2 * recs, labels), F32),
            pltpu.VMEM((heads, recs, labels), F32),
            pltpu.VMEM((2 * recs, labels), F32),
            pltpu.VMEM((n, 2 * recs, labels), F32),
            pltpu.VMEM((8, 128), F32),
            pltpu.VMEM((dp_n, 8, 128), F32),
            dma((6,)),
            dma,
            dma((half,)),
            dma((half,)),
            dma((half,)),
            dma((half,)),
            dma((half,)),
            dma((half,)),
            dma((n,)),
            dma((n,)),
            dma((n,)),
            dma((n,)),
            dma((n,)),
            dma((n,)),
            dma((dp_n,)),
            dma((dp_n,)),
        ],
        compiler_params=pltpu.CompilerParams(
            collective_id=0, has_side_effects=True, vmem_limit_bytes=48 * 1024 * 1024
        ),
    )(
        lengths,
        log_decay[0],
        label_ids,
        norm_gain.reshape(heads, hd),
        tokens[0],
        w_query,
        w_key,
        w_value,
        label_query,
        label_weight,
    )
    return (out[None], logits[None], loss, mean.reshape(()))


def solution(mesh):
    return jax.shard_map(
        local,
        mesh=mesh,
        in_specs=(
            P("dp", "ctx", None),
            P("dp", None, "ctx"),
            P("dp", None),
            P("dp", "ctx"),
            P(),
            P(),
            P(),
            P(),
            P(),
            P(),
        ),
        out_specs=(P("dp", "ctx", None), P("dp", None, None), P("dp", None), P()),
        check_vma=False,
    )
```

time: 424 us -> 52.8 us (0.12)
  waiting for transfers between devices: 127 us -> 0 us
  matrix products: 66.8 us -> 0 us
  loops' own time: 57.1 us -> 0 us
  blocking collectives: 44.8 us -> 0 us
  Pallas kernels: 0 us -> 40.3 us
  local copies, waits for them, and re-layouts: 44.4 us -> 9.69 us
  starting transfers between devices: 34.4 us -> 0 us
  other arithmetic: 29.7 us -> 0 us
  between operations: 16.6 us -> 2.47 us
    dot_general x60 -> x0, matrix products: 66.8 us -> none  [the longest x8 15 us: local_head(): intra_sum = jnp.dot(weights, v_head, preferred_element_type=jnp.float32)]
    psum x1 -> x0, waiting for transfers between devices: 64.6 us -> none  [local(): lax.psum((mass_part * rescale, weighted * rescale, counts), 'ctx')]
    ppermute x7 -> x0, waiting for transfers between devices: 62.2 us -> none  [passed_along(): return lax.ppermute(x, axis, pairs)]
    another operation x4 -> x0, loops' own time: 57.1 us -> none  [the longest x1 30.3 us: local(): lax.map(local_head, jnp.arange(head_count, dtype=jnp.int32))]
    pallas_call x0 -> x1, Pallas kernels: none -> 40.3 us  [local(): pl.pallas_call(functools.partial(fused, n, dp_n), out_shape=(jax.ShapeDty...]
    pmax x1 -> x0, blocking collectives: 38.5 us -> none  [local(): top_score = lax.pmax(maxima, 'ctx')]
    ppermute x7 -> x0, starting transfers between devices: 34.3 us -> none  [passed_along(): return lax.ppermute(x, axis, pairs)]
    dynamic_slice x56 -> x0, local copies, waits for them, and re-layouts: 28.5 us -> none  [the longest x24 14.2 us: local(): lax.map(local_head, jnp.arange(head_count, dtype=jnp.int32))]
  transfers between devices with their start and end apart: 8 -> 0, of which waited for: 8 -> 0; matrix products, arithmetic and copies ran while one was open for 0% -> 0% of each run, Pallas kernels for 0% -> 0%
where the time goes in v1:
time: 52.8 us; the launch traced here: 52.4 us
  Pallas kernels  40.3 us (76%)
  local copies, waits for them, and re-layouts  9.69 us (18%)
  between operations  2.47 us (5%)
    pallas_call x1, Pallas kernels, local(): pl.pallas_call(functools.partial(fused, n, dp_n), out_shape=(jax.ShapeDty...  40.3 us
    unnamed x19, local copies, waits for them, and re-layouts  9.69 us

profile of v1, /device:TPU:0, one launch (start us, length us, event | category | flops | bytes accessed | tf_op | source)
XLA Modules:
  0.0 52.4 jit_solution(15578781410725790079)
XLA Ops:
  0.6 0.0 copy-start
  0.6 1.6 %copy-done = bf16[1024,1024]{1,0:T(8,128)(2,1)S(1)} copy-done((bf16[1024,1024]{1,0:T(8,128)(2,1)S(1)}, bf16[1024,1024]{1,0:T(8,128)(2,1)}, u32[]{:S(2)}) %copy-start) | copy-done | bytes 2097176
  2.2 0.0 copy-start.1
  2.2 1.2 %copy-done.1 = bf16[512,1024]{1,0:T(8,128)(2,1)S(1)} copy-done((bf16[512,1024]{1,0:T(8,128)(2,1)S(1)}, bf16[512,1024]{1,0:T(8,128)(2,1)}, u32[]{:S(2)}) %copy-start.1) | copy-done | bytes 1048600
  3.5 0.0 copy-start.2
  3.5 1.2 %copy-done.2 = bf16[512,1024]{1,0:T(8,128)(2,1)S(1)} copy-done((bf16[512,1024]{1,0:T(8,128)(2,1)S(1)}, bf16[512,1024]{1,0:T(8,128)(2,1)}, u32[]{:S(2)}) %copy-start.2) | copy-done | bytes 1048600
  4.7 0.0 copy-start.3
  4.7 1.0 %copy-done.3 = bf16[1,256,1024]{2,1,0:T(8,128)(2,1)S(1)} copy-done((bf16[1,256,1024]{2,1,0:T(8,128)(2,1)S(1)}, bf16[1,256,1024]{2,1,0:T(8,128)(2,1)}, u32[]{:S(2)}) %copy-start.3) | copy-done | bytes 524312
  5.7 0.0 copy-start.4
  5.7 0.7 %copy-done.4 = f32[1,8,256]{2,1,0:T(8,128)S(1)} copy-done((f32[1,8,256]{2,1,0:T(8,128)S(1)}, f32[1,8,256]{2,1,0:T(8,128)}, u32[]{:S(2)}) %copy-start.4) | copy-done | bytes 8216
  6.4 0.0 copy-start.5
  6.4 0.7 %copy-done.5 = f32[1024]{0:T(1024)S(1)} copy-done((f32[1024]{0:T(1024)S(1)}, f32[1024]{0:T(1024)}, u32[]{:S(2)}) %copy-start.5) | copy-done | bytes 4120
  7.1 0.0 copy-start.6
  7.1 0.7 %copy-done.6 = s32[1,256]{1,0:T(1,128)S(1)} copy-done((s32[1,256]{1,0:T(1,128)S(1)}, s32[1,256]{1,0:T(1,128)}, u32[]{:S(2)}) %copy-start.6) | copy-done | bytes 1048
  7.8 0.0 copy-start.7
  7.8 0.7 %copy-done.7 = s32[1,2]{1,0:T(1,128)S(1)} copy-done((s32[1,2]{1,0:T(1,128)S(1)}, s32[1,2]{1,0:T(1,128)}, u32[]{:S(2)}) %copy-start.7) | copy-done | bytes 32
  8.4 40.3 %shard_map.129 = (bf16[256,1024]{1,0:T(8,128)(2,1)S(1)}, f32[2,512]{1,0:T(2,128)S(1)}, f32[1,2]{1,0:T(1,128)S(1)}, f32[1,1]{1,0:T(1,128)}) custom-call(s32[1,2]{1,0:T(1,128)S(1)} %copy-done.7, f32[8,256]{1,0:T(8,128)S(1)} %bitcast.8, s32[1,256]{1,0:T(1,128)S(1)} %copy-done.6, f32[8,128]{1,0:T(8,128)S(1)} %bitcast.9, bf16[256,1024]{1,0:T(8,128)(2,1)S(1)} %bitcast.6, ...), custom_call_target="tpu_custom_call" | custom-call | tf_op jit(solution)/shard_map/pallas_call | solution.py:582
  48.7 0.8 %copy.18 = bf16[1,256,1024]{2,1,0:T(8,128)(2,1)} copy(bf16[1,256,1024]{2,1,0:T(8,128)(2,1)S(1)} %bitcast.7) | data formatting | bytes 1048576
  49.5 0.6 %copy.19 = f32[1,2,512]{2,1,0:T(2,128)} copy(f32[1,2,512]{2,1,0:T(2,128)S(1)} %bitcast.10) | data formatting | bytes 8192
  50.1 0.5 copy.20
Async XLA Ops:
  0.6 1.6 %copy-start = (bf16[1024,1024]{1,0:T(8,128)(2,1)S(1)}, bf16[1024,1024]{1,0:T(8,128)(2,1)}, u32[]{:S(2)}) copy-start(bf16[1024,1024]{1,0:T(8,128)(2,1)} %wq_hbm.1) | copy-start | bytes 6291460
  2.2 1.2 %copy-start.1 = (bf16[512,1024]{1,0:T(8,128)(2,1)S(1)}, bf16[512,1024]{1,0:T(8,128)(2,1)}, u32[]{:S(2)}) copy-start(bf16[512,1024]{1,0:T(8,128)(2,1)} %lq_hbm.1) | copy-start | bytes 3145732
  3.5 1.2 %copy-start.2 = (bf16[512,1024]{1,0:T(8,128)(2,1)S(1)}, bf16[512,1024]{1,0:T(8,128)(2,1)}, u32[]{:S(2)}) copy-start(bf16[512,1024]{1,0:T(8,128)(2,1)} %lw_hbm.1) | copy-start | bytes 3145732
  4.7 1.0 %copy-start.3 = (bf16[1,256,1024]{2,1,0:T(8,128)(2,1)S(1)}, bf16[1,256,1024]{2,1,0:T(8,128)(2,1)}, u32[]{:S(2)}) copy-start(bf16[1,256,1024]{2,1,0:T(8,128)(2,1)} %param.10) | copy-start | bytes 1572868
  5.7 0.7 %copy-start.4 = (f32[1,8,256]{2,1,0:T(8,128)S(1)}, f32[1,8,256]{2,1,0:T(8,128)}, u32[]{:S(2)}) copy-start(f32[1,8,256]{2,1,0:T(8,128)} %param.11) | copy-start | bytes 24580
  6.4 0.7 %copy-start.5 = (f32[1024]{0:T(1024)S(1)}, f32[1024]{0:T(1024)}, u32[]{:S(2)}) copy-start(f32[1024]{0:T(1024)} %param.17) | copy-start | bytes 12292
  7.1 0.7 %copy-start.6 = (s32[1,256]{1,0:T(1,128)S(1)}, s32[1,256]{1,0:T(1,128)}, u32[]{:S(2)}) copy-start(s32[1,256]{1,0:T(1,128)} %label_ref.1) | copy-start | bytes 3076
  7.8 0.7 %copy-start.7 = (s32[1,2]{1,0:T(1,128)S(1)}, s32[1,2]{1,0:T(1,128)}, u32[]{:S(2)}) copy-start(s32[1,2]{1,0:T(1,128)} %lengths_ref.1) | copy-start | bytes 28

commit v2 on v1

--- a/solution.py
+++ b/solution.py
@@ -15,15 +15,16 @@
 NT = (((1,), (1,)), ((), ()))
 TN = (((0,), (0,)), ((), ()))
 PAD = 8
+VMEM_LIMIT = 63 * 1024 * 1024
 
 
 def fused(
     n,
     dp_n,
-    lengths_ref,
-    decay_ref,
-    label_ref,
-    gain_ref,
+    lengths_hbm,
+    decay_hbm,
+    label_hbm,
+    gain_hbm,
     tokens_hbm,
     wq_hbm,
     wk_hbm,
@@ -34,6 +35,10 @@
     logits_ref,
     loss_ref,
     mean_ref,
+    lengths_ref,
+    decay_ref,
+    label_ref,
+    gain_ref,
     x_ref,
     wq_ref,
     wk_ref,
@@ -95,19 +100,24 @@
     partner = me + 1 - 2 * half
     even = half == 0
 
-    loads = [
-        pltpu.make_async_copy(src, dst, in_sem.at[i])
-        for i, (src, dst) in enumerate(
-            (
-                (tokens_hbm, x_ref),
-                (wk_hbm, wk_ref),
-                (wv_hbm, wv_ref),
-                (wq_hbm, wq_ref),
-                (lq_hbm, lq_ref),
-                (lw_hbm, lw_ref),
-            )
-        )
-    ]
+    part = half_heads * hd
+    far_cols = pl.ds(pl.multiple_of((1 - half) * part, part), part)
+    near_cols = pl.ds(pl.multiple_of(half * part, part), part)
+    plan = (
+        (lengths_hbm, lengths_ref),
+        (decay_hbm, decay_ref),
+        (tokens_hbm, x_ref),
+        (wk_hbm.at[:, far_cols], wk_ref.at[0]),
+        (wv_hbm.at[:, far_cols], wv_ref.at[0]),
+        (wk_hbm.at[:, near_cols], wk_ref.at[1]),
+        (wv_hbm.at[:, near_cols], wv_ref.at[1]),
+        (wq_hbm, wq_ref),
+        (lq_hbm, lq_ref),
+        (lw_hbm, lw_ref),
+        (label_hbm, label_ref),
+        (gain_hbm, gain_ref),
+    )
+    loads = [pltpu.make_async_copy(src, dst, in_sem.at[i]) for i, (src, dst) in enumerate(plan)]
     for load in loads:
         load.start()
 
@@ -137,6 +147,8 @@
             device_id_type=pl.DeviceIdType.MESH,
         )
 
+    loads[0].wait()
+    loads[1].wait()
     shard_start = me * tok
     starts = []
     run = jnp.int32(0)
@@ -187,20 +199,15 @@
     pair_ok = (across <= down) & (col_record(tok) == row_record(tok))
     pair_bias[...] = jnp.where(pair_ok, math.log2(scale), NEG_FILL)
 
-    def project(w_ref, dst):
-        step = min(256, width)
-        for c in range(width // step):
+    def project(w_ref, dst, first):
+        columns = w_ref.shape[1]
+        step = min(256, columns)
+        for c in range(columns // step):
             res = jnp.dot(
                 x_ref[...], w_ref[:, c * step : (c + 1) * step], preferred_element_type=F32
             ).astype(BF16)
             for s in range(step // hd):
-                dst[c * (step // hd) + s] = res[:, s * hd : (s + 1) * hd]
-
-    loads[0].wait()
-    loads[1].wait()
-    project(wk_ref, k_ref)
-    loads[2].wait()
-    project(wv_ref, v_ref)
+                dst[first + c * (step // hd) + s] = res[:, s * hd : (s + 1) * hd]
 
     def local_state(h):
         cum = ccol[h]
@@ -217,6 +224,11 @@
             loc.at[h], peer_loc.at[i], loc_send.at[i], loc_recv.at[i], {"ctx": partner}
         )
 
+    loads[2].wait()
+    loads[3].wait()
+    project(wk_ref.at[0], k_ref, (1 - half) * half_heads)
+    loads[4].wait()
+    project(wv_ref.at[0], v_ref, (1 - half) * half_heads)
     pl.semaphore_wait(barrier, n - 1 + dp_n - 1)
 
     @pl.when(pair == 0)
@@ -226,6 +238,10 @@
     for i in range(half_heads):
         local_state((1 - half) * half_heads + i)
         loc_copy(i).start()
+    loads[5].wait()
+    project(wk_ref.at[1], k_ref, half * half_heads)
+    loads[6].wait()
+    project(wv_ref.at[1], v_ref, half * half_heads)
     for i in range(half_heads):
         local_state(half * half_heads + i)
 
@@ -280,8 +296,9 @@
         hand_copy(i).start()
         state[h] = jnp.where(even, came, middle)
 
-    units = 2 * heads
-    first_unit = jnp.minimum(1 + 3 * pair, units - half_heads)
+    group = 2
+    units = heads + heads // group
+    first_unit = jnp.minimum(1 + (7 * pair) // 2, units)
 
     def maybe_chain(unit):
         i = unit - first_unit
@@ -290,9 +307,9 @@
         def _():
             chain_step(i)
 
-    loads[3].wait()
-    project(wq_ref, q_ref)
-    loads[4].wait()
+    loads[7].wait()
+    project(wq_ref, q_ref, 0)
+    loads[8].wait()
 
     chunk = min(256, labels)
 
@@ -365,12 +382,13 @@
         weights = (scores * fade).astype(BF16)
         intra[h] = jnp.dot(weights, v_ref[h], preferred_element_type=F32)
 
-    def intra_body(h, _):
-        intra_unit(h)
-        maybe_chain(heads + h)
+    def intra_body(u, _):
+        for s in range(group):
+            intra_unit(u * group + s)
+        maybe_chain(heads + u)
         return 0
 
-    lax.fori_loop(0, heads, intra_body, 0)
+    lax.fori_loop(0, heads // group, intra_body, 0)
 
     def lse_copy(d):
         return send(
@@ -404,6 +422,7 @@
         lse[lax.rem(me, heads)] = top + jnp.log(mass) * LOG2E
         each_peer(lambda d: lse_copy(d).start())
 
+    loads[10].wait()
     hot = (
         lax.broadcasted_iota(jnp.int32, (labels, tok), 0) == label_ref[...]
     ).astype(F32).astype(BF16)
@@ -413,7 +432,8 @@
     counts = lax.dot_general(members, hot, NT, preferred_element_type=F32)
     contrib[recs:, :] = counts[:recs, :]
 
-    loads[5].wait()
+    loads[9].wait()
+    loads[11].wait()
 
     def finish(h):
         lanes = pl.ds(pl.multiple_of(h * hd, hd), hd)
@@ -444,17 +464,19 @@
                     jnp.where(rec == r, value, 0.0), axis=0, keepdims=True
                 )
 
-    def finish_own(i, _):
-        finish(half * half_heads + i)
-        return 0
-
-    def finish_other(i, _):
-        hand_arrival(i).wait_recv()
-        finish((1 - half) * half_heads + i)
-        return 0
-
-    lax.fori_loop(0, half_heads, finish_own, 0)
-    lax.fori_loop(0, half_heads, finish_other, 0)
+    for i in range(half_heads + 1):
+        if i < half_heads:
+
+            @pl.when(first_unit + i >= units)
+            def _():
+                chain_step(i)
+
+        if i > 0:
+            hand_arrival(i - 1).wait_recv()
+        if i < half_heads:
+            finish(half * half_heads + i)
+        if i > 0:
+            finish((1 - half) * half_heads + i - 1)
 
     store = pltpu.make_async_copy(out_buf, out_hbm, out_sem)
     store.start()
@@ -552,6 +574,15 @@
             chain_copy(i).wait_send()
 
     store.wait()
+
+
+def write_out(*refs):
+    sems = refs[8]
+    copies = [pltpu.make_async_copy(refs[i], refs[4 + i], sems.at[i]) for i in range(4)]
+    for copy in copies:
+        copy.start()
+    for copy in copies:
+        copy.wait()
 
 
 def local(
@@ -576,24 +607,29 @@
     half = heads // 2
     assert n >= heads and n % 2 == 0
     any_space = pl.BlockSpec(memory_space=pl.ANY)
+    hbm = pl.BlockSpec(memory_space=pltpu.HBM)
     vmem = pl.BlockSpec(memory_space=pltpu.VMEM)
-    smem = pl.BlockSpec(memory_space=pltpu.SMEM)
     dma = pltpu.SemaphoreType.DMA
-    out, logits, loss, mean = pl.pallas_call(
+    out_shape = (
+        jax.ShapeDtypeStruct((tok, width), BF16),
+        jax.ShapeDtypeStruct((recs, labels), F32),
+        jax.ShapeDtypeStruct((1, recs), F32),
+        jax.ShapeDtypeStruct((1, 1), F32),
+    )
+    results = pl.pallas_call(
         functools.partial(fused, n, dp_n),
-        out_shape=(
-            jax.ShapeDtypeStruct((tok, width), BF16),
-            jax.ShapeDtypeStruct((recs, labels), F32),
-            jax.ShapeDtypeStruct((1, recs), F32),
-            jax.ShapeDtypeStruct((1, 1), F32),
-        ),
-        in_specs=[smem, vmem, vmem, vmem] + [any_space] * 6,
-        out_specs=(any_space, vmem, vmem, vmem),
+        out_shape=out_shape,
+        in_specs=[hbm] * 10,
+        out_specs=(hbm,) + (vmem,) * 3,
         scratch_shapes=[
+            pltpu.SMEM((1, recs), jnp.int32),
+            pltpu.VMEM((heads, tok), F32),
+            pltpu.VMEM((1, tok), jnp.int32),
+            pltpu.VMEM((heads, hd), F32),
             pltpu.VMEM((tok, width), BF16),
             pltpu.VMEM((width, width), BF16),
-            pltpu.VMEM((width, width), BF16),
-            pltpu.VMEM((width, width), BF16),
+            pltpu.VMEM((2, width, width // 2), BF16),
+            pltpu.VMEM((2, width, width // 2), BF16),
             pltpu.VMEM((labels, width), BF16),
             pltpu.VMEM((labels, width), BF16),
             pltpu.VMEM((heads, tok, hd), BF16),
@@ -619,7 +655,7 @@
             pltpu.VMEM((n, 2 * recs, labels), F32),
             pltpu.VMEM((8, 128), F32),
             pltpu.VMEM((dp_n, 8, 128), F32),
-            dma((6,)),
+            dma((12,)),
             dma,
             dma((half,)),
             dma((half,)),
@@ -637,7 +673,7 @@
             dma((dp_n,)),
         ],
         compiler_params=pltpu.CompilerParams(
-            collective_id=0, has_side_effects=True, vmem_limit_bytes=48 * 1024 * 1024
+            collective_id=0, has_side_effects=True, vmem_limit_bytes=VMEM_LIMIT
         ),
     )(
         lengths,
@@ -651,6 +687,14 @@
         label_query,
         label_weight,
     )
+    out, logits, loss, mean = pl.pallas_call(
+        write_out,
+        out_shape=out_shape,
+        in_specs=[any_space] * 4,
+        out_specs=(hbm,) * 4,
+        scratch_shapes=[dma((4,))],
+        compiler_params=pltpu.CompilerParams(vmem_limit_bytes=VMEM_LIMIT),
+    )(*results)
     return (out[None], logits[None], loss, mean.reshape(()))
 
 

time: 52.8 us -> 59.5 us (1.13)
  Pallas kernels: 40.3 us -> 58.7 us
  local copies, waits for them, and re-layouts: 9.69 us -> 0 us
  between operations: 2.47 us -> 0.64 us
    pallas_call x1 -> x2, Pallas kernels: 40.3 us -> 58.7 us  [the longest x1 41 us: local(): pl.pallas_call(functools.partial(fused, n, dp_n), out_shape=out_shape, in...]
    unnamed x19 -> x0, local copies, waits for them, and re-layouts: 9.69 us -> none
where the time goes in v2:
time: 59.5 us; the launch traced here: 59.4 us
  Pallas kernels  58.7 us (99%)
  between operations  0.64 us (1%)
    pallas_call x1, Pallas kernels, local(): pl.pallas_call(functools.partial(fused, n, dp_n), out_shape=out_shape, in...  41 us
    pallas_call x1, Pallas kernels, local(): pl.pallas_call(write_out, out_shape=out_shape, in_specs=[any_space] * 4,...  17.7 us

profile of v2, /device:TPU:0, one launch (start us, length us, event | category | flops | bytes accessed | tf_op | source)
XLA Modules:
  0.0 59.4 jit_solution(13405505880199405998)
XLA Ops:
  0.6 41.0 %shard_map.129 = (bf16[256,1024]{1,0:T(8,128)(2,1)}, f32[2,512]{1,0:T(2,128)}, f32[1,2]{1,0:T(1,128)}, f32[1,1]{1,0:T(1,128)}) custom-call(s32[1,2]{1,0:T(1,128)} %lengths_hbm.1, f32[8,256]{1,0:T(8,128)} %bitcast.7, s32[1,256]{1,0:T(1,128)} %label_hbm.1, f32[8,128]{1,0:T(8,128)} %bitcast.8, bf16[256,1024]{1,0:T(8,128)(2,1)} %bitcast.6, ...), custom_call_target="tpu_custom_call" | custom-call | tf_op jit(solution)/shard_map/pallas_call | solution.py:619
  41.6 17.7 %shard_map.130 = (bf16[256,1024]{1,0:T(8,128)(2,1)}, f32[2,512]{1,0:T(2,128)}, f32[1,2]{1,0:T(1,128)}, f32[1,1]{1,0:T(1,128)}) custom-call(bf16[256,1024]{1,0:T(8,128)(2,1)} %get-tuple-element.12.refs_0_, f32[2,512]{1,0:T(2,128)} %get-tuple-element.13.refs_1_, f32[1,2]{1,0:T(1,128)} %get-tuple-element.14.refs_2_, f32[1,1]{1,0:T(1,128)} %get-tuple-element.15.refs_3_), custom_call_target="tpu_custom_call" | custom-call | tf_op jit(solution)/shard_map/pallas_call | solution.py:690

commit v3 on v2

--- a/solution.py
+++ b/solution.py
@@ -15,6 +15,7 @@
 NT = (((1,), (1,)), ((), ()))
 TN = (((0,), (0,)), ((), ()))
 PAD = 8
+PIECES = 2
 VMEM_LIMIT = 63 * 1024 * 1024
 
 
@@ -118,7 +119,7 @@
         (gain_hbm, gain_ref),
     )
     loads = [pltpu.make_async_copy(src, dst, in_sem.at[i]) for i, (src, dst) in enumerate(plan)]
-    for load in loads:
+    for load in loads[:5]:
         load.start()
 
     barrier = pltpu.get_barrier_semaphore()
@@ -209,25 +210,37 @@
             for s in range(step // hd):
                 dst[first + c * (step // hd) + s] = res[:, s * hd : (s + 1) * hd]
 
+    piece = hd // PIECES
+
     def local_state(h):
         cum = ccol[h]
         last = cum[tok - 1 : tok, :]
         fade = jnp.exp2(jnp.where(col_record(hd) == last_rec, last - cum, NEG_FILL))
         kdec = (k_ref[h].astype(F32) * fade).astype(BF16)
-        loc[h, :hd, :] = lax.dot_general(kdec, v_ref[h], TN, preferred_element_type=F32)
+        made = lax.dot_general(kdec, v_ref[h], TN, preferred_element_type=F32)
         carry = jnp.where(last_rec == before_rec, jnp.exp2(last), 0.0)
-        loc[h, hd:, :] = jnp.broadcast_to(carry, (PAD, hd))
-
-    def loc_copy(i):
+        for s in range(PIECES):
+            loc[h, s, :piece, :] = made[s * piece : (s + 1) * piece, :]
+            loc[h, s, piece:, :] = jnp.broadcast_to(carry, (PAD, hd))
+
+    def loc_copy(i, s):
         h = (1 - half) * half_heads + i
         return send(
-            loc.at[h], peer_loc.at[i], loc_send.at[i], loc_recv.at[i], {"ctx": partner}
+            loc.at[h, s],
+            peer_loc.at[i, s],
+            loc_send.at[i, s],
+            loc_recv.at[i, s],
+            {"ctx": partner},
         )
 
     loads[2].wait()
     loads[3].wait()
+    for load in loads[5:7]:
+        load.start()
     project(wk_ref.at[0], k_ref, (1 - half) * half_heads)
     loads[4].wait()
+    for load in loads[7:]:
+        load.start()
     project(wv_ref.at[0], v_ref, (1 - half) * half_heads)
     pl.semaphore_wait(barrier, n - 1 + dp_n - 1)
 
@@ -237,7 +250,57 @@
 
     for i in range(half_heads):
         local_state((1 - half) * half_heads + i)
-        loc_copy(i).start()
+        for s in range(PIECES):
+            loc_copy(i, s).start()
+    def chain_copy(i, s):
+        return send(
+            chain_out.at[i, s],
+            chain_in.at[i, s],
+            chain_send.at[i, s],
+            chain_recv.at[i, s],
+            {"ctx": lax.rem(me + 2, n)},
+        )
+
+    def hand_to(i, s, h):
+        return send(
+            hand.at[i, s],
+            state.at[h, s],
+            hand_send.at[i, s],
+            hand_recv.at[i, s],
+            {"ctx": partner},
+        )
+
+    def hand_copy(i, s):
+        return hand_to(i, s, half * half_heads + i)
+
+    def hand_arrival(i, s):
+        return hand_to(i, s, (1 - half) * half_heads + i)
+
+    def chain_step(i):
+        h = half * half_heads + i
+        for s in range(PIECES):
+            loc_copy(i, s).wait_recv()
+
+            @pl.when(pair > 0)
+            def _():
+                chain_copy(i, s).wait_recv()
+
+            came = chain_in[i, s]
+            own = loc[h, s]
+            other = peer_loc[i, s]
+            first = jnp.where(even, own, other)
+            second = jnp.where(even, other, own)
+            middle = first[piece : piece + 1, :] * came + first[:piece, :]
+
+            @pl.when(pair < pairs - 1)
+            def _():
+                chain_out[i, s] = second[piece : piece + 1, :] * middle + second[:piece, :]
+                chain_copy(i, s).start()
+
+            hand[i, s] = jnp.where(even, middle, came)
+            hand_copy(i, s).start()
+            state[h, s] = jnp.where(even, came, middle)
+
     loads[5].wait()
     project(wk_ref.at[1], k_ref, half * half_heads)
     loads[6].wait()
@@ -245,60 +308,13 @@
     for i in range(half_heads):
         local_state(half * half_heads + i)
 
-    def chain_copy(i):
-        return send(
-            chain_out.at[i],
-            chain_in.at[i],
-            chain_send.at[i],
-            chain_recv.at[i],
-            {"ctx": lax.rem(me + 2, n)},
-        )
-
-    def hand_copy(i):
-        return send(
-            hand.at[i],
-            state.at[half * half_heads + i],
-            hand_send.at[i],
-            hand_recv.at[i],
-            {"ctx": partner},
-        )
-
-    def hand_arrival(i):
-        return send(
-            hand.at[i],
-            state.at[(1 - half) * half_heads + i],
-            hand_send.at[i],
-            hand_recv.at[i],
-            {"ctx": partner},
-        )
-
-    def chain_step(i):
-        h = half * half_heads + i
-        loc_copy(i).wait_recv()
-
-        @pl.when(pair > 0)
+        @pl.when(pair == 0)
         def _():
-            chain_copy(i).wait_recv()
-
-        came = chain_in[i]
-        own = loc[h]
-        other = peer_loc[i]
-        first = jnp.where(even, own, other)
-        second = jnp.where(even, other, own)
-        middle = first[hd : hd + 1, :] * came + first[:hd, :]
-
-        @pl.when(pair < pairs - 1)
-        def _():
-            chain_out[i] = second[hd : hd + 1, :] * middle + second[:hd, :]
-            chain_copy(i).start()
-
-        hand[i] = jnp.where(even, middle, came)
-        hand_copy(i).start()
-        state[h] = jnp.where(even, came, middle)
+            chain_step(i)
 
     group = 2
     units = heads + heads // group
-    first_unit = jnp.minimum(1 + (7 * pair) // 2, units)
+    first_unit = jnp.where(pair == 0, -half_heads, jnp.minimum(4 * pair - 3, units))
 
     def maybe_chain(unit):
         i = unit - first_unit
@@ -437,7 +453,7 @@
 
     def finish(h):
         lanes = pl.ds(pl.multiple_of(h * hd, hd), hd)
-        st = state[h]
+        st = jnp.concatenate([state[h, s] for s in range(PIECES)], axis=0)
         high = st.astype(BF16)
         low = (st - high.astype(F32)).astype(BF16)
         q = q_ref[h]
@@ -472,7 +488,8 @@
                 chain_step(i)
 
         if i > 0:
-            hand_arrival(i - 1).wait_recv()
+            for s in range(PIECES):
+                hand_arrival(i - 1, s).wait_recv()
         if i < half_heads:
             finish(half * half_heads + i)
         if i > 0:
@@ -565,24 +582,35 @@
 
     each_peer(end_stat)
     for i in range(half_heads):
-        loc_copy(i).wait_send()
-        hand_copy(i).wait_send()
+        for s in range(PIECES):
+            loc_copy(i, s).wait_send()
+            hand_copy(i, s).wait_send()
 
     @pl.when(pair < pairs - 1)
     def _():
         for i in range(half_heads):
-            chain_copy(i).wait_send()
+            for s in range(PIECES):
+                chain_copy(i, s).wait_send()
 
     store.wait()
 
 
 def write_out(*refs):
-    sems = refs[8]
-    copies = [pltpu.make_async_copy(refs[i], refs[4 + i], sems.at[i]) for i in range(4)]
-    for copy in copies:
-        copy.start()
-    for copy in copies:
-        copy.wait()
+    ins, outs, held, sems = refs[:4], refs[4:8], refs[8:12], refs[12]
+    rows = ins[0].shape[0] // 2
+    pieces = [(i, ins[i], outs[i], held[i]) for i in range(1, 4)]
+    for p in range(2):
+        cut = pl.ds(p * rows, rows)
+        pieces.append((4 * p, ins[0].at[cut], outs[0].at[cut], held[0].at[cut]))
+    fetches = [pltpu.make_async_copy(src, mid, sems.at[0, i]) for i, src, dst, mid in pieces]
+    stores = [pltpu.make_async_copy(mid, dst, sems.at[1, i]) for i, src, dst, mid in pieces]
+    for fetch in fetches:
+        fetch.start()
+    for fetch, store in zip(fetches, stores):
+        fetch.wait()
+        store.start()
+    for store in stores:
+        store.wait()
 
 
 def local(
@@ -605,6 +633,7 @@
     recs = lengths.shape[1]
     labels = label_query.shape[0]
     half = heads // 2
+    piece = hd // PIECES
     assert n >= heads and n % 2 == 0
     any_space = pl.BlockSpec(memory_space=pl.ANY)
     hbm = pl.BlockSpec(memory_space=pltpu.HBM)
@@ -642,12 +671,12 @@
             pltpu.VMEM((heads, tok, labels), F32),
             pltpu.VMEM((heads, recs, labels), F32),
             pltpu.VMEM((tok, width), BF16),
-            pltpu.VMEM((heads, hd + PAD, hd), F32),
-            pltpu.VMEM((half, hd + PAD, hd), F32),
-            pltpu.VMEM((half, hd, hd), F32),
-            pltpu.VMEM((half, hd, hd), F32),
-            pltpu.VMEM((half, hd, hd), F32),
-            pltpu.VMEM((heads, hd, hd), F32),
+            pltpu.VMEM((heads, PIECES, piece + PAD, hd), F32),
+            pltpu.VMEM((half, PIECES, piece + PAD, hd), F32),
+            pltpu.VMEM((half, PIECES, piece, hd), F32),
+            pltpu.VMEM((half, PIECES, piece, hd), F32),
+            pltpu.VMEM((half, PIECES, piece, hd), F32),
+            pltpu.VMEM((heads, PIECES, piece, hd), F32),
             pltpu.VMEM((heads, 2 * recs, labels), F32),
             pltpu.VMEM((n, 2 * recs, labels), F32),
             pltpu.VMEM((heads, recs, labels), F32),
@@ -657,12 +686,12 @@
             pltpu.VMEM((dp_n, 8, 128), F32),
             dma((12,)),
             dma,
-            dma((half,)),
-            dma((half,)),
-            dma((half,)),
-            dma((half,)),
-            dma((half,)),
-            dma((half,)),
+            dma((half, PIECES)),
+            dma((half, PIECES)),
+            dma((half, PIECES)),
+            dma((half, PIECES)),
+            dma((half, PIECES)),
+            dma((half, PIECES)),
             dma((n,)),
             dma((n,)),
             dma((n,)),
@@ -692,7 +721,7 @@
         out_shape=out_shape,
         in_specs=[any_space] * 4,
         out_specs=(hbm,) * 4,
-        scratch_shapes=[dma((4,))],
+        scratch_shapes=[pltpu.VMEM(o.shape, o.dtype) for o in out_shape] + [dma((2, 5))],
         compiler_params=pltpu.CompilerParams(vmem_limit_bytes=VMEM_LIMIT),
     )(*results)
     return (out[None], logits[None], loss, mean.reshape(()))

time: 59.5 us -> 43 us (0.72)
  Pallas kernels: 58.7 us -> 42.2 us
    pallas_call x1, Pallas kernels: 17.7 us -> 2.39 us  [local(): pl.pallas_call(write_out, out_shape=out_shape, in_specs=[any_space] * 4,...]
    pallas_call x1, Pallas kernels: 41 us -> 39.8 us  [local(): pl.pallas_call(functools.partial(fused, n, dp_n), out_shape=out_shape, in...]
where the time goes in v3:
time: 43 us; the launch traced here: 42.8 us
  Pallas kernels  42.2 us (98%)
  between operations  0.64 us (1%)
    pallas_call x1, Pallas kernels, local(): pl.pallas_call(functools.partial(fused, n, dp_n), out_shape=out_shape, in...  39.8 us
    pallas_call x1, Pallas kernels, local(): pl.pallas_call(write_out, out_shape=out_shape, in_specs=[any_space] * 4,...  2.39 us

profile of v3, /device:TPU:0, one launch (start us, length us, event | category | flops | bytes accessed | tf_op | source)
XLA Modules:
  0.0 42.8 jit_solution(15087675758171107048)
XLA Ops:
  0.6 39.8 %shard_map.129 = (bf16[256,1024]{1,0:T(8,128)(2,1)}, f32[2,512]{1,0:T(2,128)}, f32[1,2]{1,0:T(1,128)}, f32[1,1]{1,0:T(1,128)}) custom-call(s32[1,2]{1,0:T(1,128)} %lengths_hbm.1, f32[8,256]{1,0:T(8,128)} %bitcast.7, s32[1,256]{1,0:T(1,128)} %label_hbm.1, f32[8,128]{1,0:T(8,128)} %bitcast.8, bf16[256,1024]{1,0:T(8,128)(2,1)} %bitcast.6, ...), custom_call_target="tpu_custom_call" | custom-call | tf_op jit(solution)/shard_map/pallas_call | solution.py:648
  40.4 2.4 %shard_map.130 = (bf16[256,1024]{1,0:T(8,128)(2,1)}, f32[2,512]{1,0:T(2,128)}, f32[1,2]{1,0:T(1,128)}, f32[1,1]{1,0:T(1,128)}) custom-call(bf16[256,1024]{1,0:T(8,128)(2,1)} %get-tuple-element.12.refs_0_, f32[2,512]{1,0:T(2,128)} %get-tuple-element.13.refs_1_, f32[1,2]{1,0:T(1,128)} %get-tuple-element.14.refs_2_, f32[1,1]{1,0:T(1,128)} %get-tuple-element.15.refs_3_), custom_call_target="tpu_custom_call" | custom-call | tf_op jit(solution)/shard_map/pallas_call | solution.py:719

commit v4 on v3

--- a/solution.py
+++ b/solution.py
@@ -328,6 +328,9 @@
     loads[8].wait()
 
     chunk = min(256, labels)
+    members = (
+        row_record(16) == lax.broadcasted_iota(jnp.int32, (16, tok), 0)
+    ).astype(F32).astype(BF16)
 
     def pool_unit(h):
         lanes = pl.ds(pl.multiple_of(h * hd, hd), hd)
@@ -344,13 +347,12 @@
             top = tops[0]
             for r in range(1, recs):
                 top = jnp.where(rec == r, tops[r], top)
-            weight = jnp.exp2((scores - top) * soft)
+            weight = jnp.exp2((scores - top) * soft).astype(BF16)
             pool_w[h, :, cols] = weight
             for r in range(recs):
                 stats[h, r : r + 1, cols] = tops[r] * soft
-                stats[h, recs + r : recs + r + 1, cols] = jnp.sum(
-                    jnp.where(rec == r, weight, 0.0), axis=0, keepdims=True
-                )
+            mass = jnp.dot(members, weight, preferred_element_type=F32)
+            stats[h, recs:, cols] = mass[:recs, :]
 
     def pool_body(h, _):
         pool_unit(h)
@@ -442,9 +444,6 @@
     hot = (
         lax.broadcasted_iota(jnp.int32, (labels, tok), 0) == label_ref[...]
     ).astype(F32).astype(BF16)
-    members = (
-        row_record(16) == lax.broadcasted_iota(jnp.int32, (16, tok), 0)
-    ).astype(F32).astype(BF16)
     counts = lax.dot_general(members, hot, NT, preferred_element_type=F32)
     contrib[recs:, :] = counts[:recs, :]
 
@@ -470,15 +469,11 @@
         variance = jnp.mean(centred * centred, axis=1, keepdims=True)
         rows = (centred * lax.rsqrt(variance + 1e-05) * gain_ref[pl.ds(h, 1), :]).astype(BF16)
         out_buf[:, lanes] = rows
-        rec = col_record(chunk)
         for c in range(labels // chunk):
             cols = slice(c * chunk, (c + 1) * chunk)
             value = lax.dot_general(rows, lw_ref[cols, lanes], NT, preferred_element_type=F32)
-            value = value * pool_w[h, :, cols]
-            for r in range(recs):
-                weighted[h, r : r + 1, cols] = jnp.sum(
-                    jnp.where(rec == r, value, 0.0), axis=0, keepdims=True
-                )
+            value = (value * pool_w[h, :, cols].astype(F32)).astype(BF16)
+            weighted[h, :, cols] = jnp.dot(members, value, preferred_element_type=F32)[:recs, :]
 
     for i in range(half_heads + 1):
         if i < half_heads:
@@ -668,7 +663,7 @@
             pltpu.VMEM((heads, 1, tok), F32),
             pltpu.VMEM((tok, tok), F32),
             pltpu.VMEM((heads, tok, hd), F32),
-            pltpu.VMEM((heads, tok, labels), F32),
+            pltpu.VMEM((heads, tok, labels), BF16),
             pltpu.VMEM((heads, recs, labels), F32),
             pltpu.VMEM((tok, width), BF16),
             pltpu.VMEM((heads, PIECES, piece + PAD, hd), F32),

time: 43 us -> 46.4 us (1.079)
  Pallas kernels: 42.2 us -> 45.6 us
    pallas_call x1, Pallas kernels: 39.8 us -> 43.2 us  [local(): pl.pallas_call(functools.partial(fused, n, dp_n), out_shape=out_shape, in...]
where the time goes in v4:
time: 46.4 us; the launch traced here: 46.2 us
  Pallas kernels  45.6 us (98%)
  between operations  0.64 us (1%)
    pallas_call x1, Pallas kernels, local(): pl.pallas_call(functools.partial(fused, n, dp_n), out_shape=out_shape, in...  43.2 us
    pallas_call x1, Pallas kernels, local(): pl.pallas_call(write_out, out_shape=out_shape, in_specs=[any_space] * 4,...  2.39 us

profile of v4, /device:TPU:0, one launch (start us, length us, event | category | flops | bytes accessed | tf_op | source)
XLA Modules:
  0.0 46.2 jit_solution(7130775437880085700)
XLA Ops:
  0.6 43.2 %shard_map.129 = (bf16[256,1024]{1,0:T(8,128)(2,1)}, f32[2,512]{1,0:T(2,128)}, f32[1,2]{1,0:T(1,128)}, f32[1,1]{1,0:T(1,128)}) custom-call(s32[1,2]{1,0:T(1,128)} %lengths_hbm.1, f32[8,256]{1,0:T(8,128)} %bitcast.7, s32[1,256]{1,0:T(1,128)} %label_hbm.1, f32[8,128]{1,0:T(8,128)} %bitcast.8, bf16[256,1024]{1,0:T(8,128)(2,1)} %bitcast.6, ...), custom_call_target="tpu_custom_call" | custom-call | tf_op jit(solution)/shard_map/pallas_call | solution.py:643
  43.9 2.4 %shard_map.130 = (bf16[256,1024]{1,0:T(8,128)(2,1)}, f32[2,512]{1,0:T(2,128)}, f32[1,2]{1,0:T(1,128)}, f32[1,1]{1,0:T(1,128)}) custom-call(bf16[256,1024]{1,0:T(8,128)(2,1)} %get-tuple-element.12.refs_0_, f32[2,512]{1,0:T(2,128)} %get-tuple-element.13.refs_1_, f32[1,2]{1,0:T(1,128)} %get-tuple-element.14.refs_2_, f32[1,1]{1,0:T(1,128)} %get-tuple-element.15.refs_3_), custom_call_target="tpu_custom_call" | custom-call | tf_op jit(solution)/shard_map/pallas_call | solution.py:714
